TPU v7x, 256 devices: a whole 4x4x8 slice. The times are simulated.
256 devices in a mesh: example: 64 (over x, z, core), feature: 4 (over y).
Axes of the slice: x: 4, y: 4, z: 8, core: 2. Of those that a mesh axis runs over, the one named last changes fastest.
Arguments:
- embeddings: bfloat16 [36864, 16384], P('example', 'feature'), may hold values from -16 to 16
- subspace: bfloat16 [16384, 128], P('feature'), may hold values from -0.046875 to 0.046875
- noise_levels: int32 [16384, 128], P('feature'), may hold values from -16 to 16
- targets: int32 [2048], replicated, may hold values from 0 to 16383
Outputs:
- embedding_grad: bfloat16 [36864, 16384], P('example', 'feature')
All inputs are finite; a program needn't handle non-finite values.
Results may differ from a plain program's by a relative error of at most 0.0085.
Values may be sent and summed in bfloat16 or wider, within the bound.
A program may use at most 64 MiB of HBM per device.

v0:
```python
import jax
import jax.numpy as jnp
from jax import lax
from jax.sharding import PartitionSpec as P

NOISE_STEP = 1.0 / 4096.0
HIGH = lax.Precision.HIGHEST


def transposed(former, latter, precision=None):
    return lax.dot_general(
        former,
        latter,
        (((0,), (0,)), ((), ())),
        precision=precision,
        preferred_element_type=jnp.float32,
    )


def by_columns(former, latter):
    return lax.dot_general(
        former, latter, (((1,), (1,)), ((), ())), preferred_element_type=jnp.float32
    )


def count_rows(targets, first, length):
    local = targets - first
    inside = (local >= 0) & (local < length)
    slots = jnp.where(inside, local, length)
    ones = jnp.ones(targets.shape, jnp.float32)
    return jax.ops.segment_sum(ones, slots, num_segments=length + 1)[:length]


def upper_factor(gram_matrix):
    return jnp.linalg.cholesky(gram_matrix).T


def factorize(gram_matrix):
    lower_factor = jnp.linalg.cholesky(gram_matrix)
    identity = jnp.eye(gram_matrix.shape[0], dtype=jnp.float32)
    inverse_factor = jax.scipy.linalg.solve_triangular(lower_factor, identity, lower=True)
    gram_inverse = jnp.dot(inverse_factor.T, inverse_factor, precision=HIGH)
    return (inverse_factor, gram_inverse)


def on_device(embeddings, subspace, noise_levels, targets):
    row_count, local_width = embeddings.shape
    examples = lax.axis_size("example")
    total_rows = row_count * examples
    projected = lax.psum(
        jnp.dot(embeddings, subspace, preferred_element_type=jnp.float32), "feature"
    )
    projected_low = projected.astype(jnp.bfloat16)
    feature_first = lax.axis_index("feature") * local_width
    share = local_width // examples
    summed = lax.psum_scatter(
        transposed(embeddings, projected_low), "example", scatter_dimension=0, tiled=True
    )
    offset = lax.axis_index("example") * share
    noise_part = lax.dynamic_slice_in_dim(noise_levels, offset, share, 0)
    image = summed / total_rows + NOISE_STEP * noise_part.astype(jnp.float32)
    row_counts = count_rows(targets, feature_first + offset, share)
    gram_matrix = lax.psum(transposed(image, image, HIGH), ("example", "feature"))
    inverse_factor, gram_inverse = factorize(gram_matrix)
    orthonormal = jnp.dot(image, inverse_factor.T, precision=HIGH)
    alignment = lax.psum(
        transposed(orthonormal * row_counts[:, None], orthonormal, HIGH), ("example", "feature")
    )
    factor_grad = 2.0 * jnp.dot(alignment, inverse_factor, precision=HIGH)
    unused, pull_back = jax.vjp(upper_factor, gram_matrix)
    gram_grad = pull_back(factor_grad)[0]
    image_grad = jnp.dot(image, gram_grad + gram_grad.T, precision=HIGH) - 2.0 * row_counts[
        :, None
    ] * jnp.dot(image, gram_inverse, precision=HIGH)
    grad_low = image_grad.astype(jnp.bfloat16)
    grad_low = lax.all_gather(grad_low, "example", axis=0, tiled=True)
    back_sum = lax.psum(
        jnp.dot(embeddings, grad_low, preferred_element_type=jnp.float32), "feature"
    )
    back_rows = back_sum.astype(jnp.bfloat16)
    result = by_columns(projected_low, grad_low) + by_columns(back_rows, subspace)
    return result.astype(jnp.bfloat16)


def solution(mesh):
    in_specs = (P("example", "feature"), P("feature", None), P("feature", None), P())
    out_specs = P("example", "feature")
    return jax.shard_map(
        on_device, mesh=mesh, in_specs=in_specs, out_specs=out_specs, check_vma=False
    )
```

profile of v0, /device:TPU:1, one launch (start us, length us, event | category | flops | bytes accessed | tf_op | source)
XLA Modules:
  0.0 795.4 jit_solution(3288870860719686440)
XLA Ops:
  6.5 4.2 fusion.45
  10.7 17.6 %all-reduce.8 = bf16[576,128]{1,0:T(8,128)(2,1)S(1)} all-reduce(f32[576,128]{1,0:T(8,128)S(1)} %fusion.45), channel_id=1, replica_groups=mesh['example'=64,'feature'=4] {'feature'}, use_global_device_ids=true, to_apply=%region_0.0 | all-reduce | flops 73728 | bytes 442368 | tf_op jit(solution)/shard_map/psum | solution.py:50
  28.3 4.7 convolution_bitcast_fusion
  33.0 2.9 copy.14
  36.2 14.7 %scatter_custom_fusion = f32[65]{0:T(128)S(1)} fusion(s32[2048]{0:T(1024)S(1)} %and_select_fusion, f32[2048]{0:T(1024)S(1)} %broadcast.95, f32[]{:T(128)} %constant.76.clone.1), kind=kCustom, calls=%fused_computation.59 | custom fusion | flops 2048 | bytes 264 | tf_op jit(solution)/shard_map/scatter-add | solution.py:31
  50.8 125.1 %reduce-scatter.4.cloned.1.call-done = f32[64,128]{1,0:T(8,128)} async-done(((f32[4096,128]{1,0:T(8,128)}), f32[64,128]{1,0:T(8,128)}) %reduce-scatter.4.cloned.1.call-update) | async-done | bytes 32784
  176.0 0.8 copy.15
  176.9 0.9 fusion.46
  177.8 246.1 %all-reduce.5.cloned.1.call-done = f32[128,128]{0,1:T(8,128)} async-done(((f32[128,128]{0,1:T(8,128)}), f32[128,128]{0,1:T(8,128)}) %all-reduce.5.cloned.1.call-update) | async-done | bytes 65552 | tf_op jit(solution)/shard_map/psum | solution.py:63
  424.0 0.9 copy.11
  424.9 0.9 fusion.22
  425.8 11.7 %custom-call.14 = f32[128,128]{1,0:T(8,128)S(1)} custom-call(f32[128,128]{1,0:T(8,128)S(1)} %fusion.22), custom_call_target="Cholesky" | custom-call | tf_op jit(solution)/shard_map/jvp(jit(cholesky))/cholesky/custom-call.1 | solution.py:35
  437.5 0.7 compare_reduce_fusion
  438.8 9.8 %custom-call.13 = f32[1,128,128]{1,2,0:T(8,128)S(1)} custom-call(f32[1,128,128]{2,1,0:T(8,128)S(1)} %fusion.24), custom_call_target="InvertDiagBlocksLowerTriangular" | custom-call | tf_op jit(solution)/shard_map/transpose(jvp(jit(cholesky)))/triangular_solve | solution.py:35
  449.2 1.0 fusion.29
  450.7 233.9 %all-reduce.7.cloned.1.call-done = f32[128,128]{1,0:T(8,128)} async-done(((f32[128,128]{1,0:T(8,128)}), f32[128,128]{1,0:T(8,128)}) %all-reduce.7.cloned.1.call-update) | async-done | bytes 65552 | tf_op jit(solution)/shard_map/psum | solution.py:66
  684.6 1.1 fusion.1
  685.7 0.9 fusion
  687.5 0.9 fusion.3
  688.4 73.0 %all-gather.2.cloned.1.call-done = bf16[4096,128]{1,0:T(8,128)(2,1)} async-done(((bf16[64,128]{1,0:T(8,128)(2,1)}), bf16[4096,128]{1,0:T(8,128)(2,1)}) %all-gather.2.cloned.1.call-update) | async-done | bytes 1048592 | tf_op jit(solution)/shard_map/all_gather | solution.py:76
  761.4 5.2 convolution_bitcast_fusion.1
  766.6 17.2 %all-reduce.9 = bf16[576,128]{0,1:T(8,128)(2,1)S(1)} all-reduce(f32[576,128]{0,1:T(8,128)} %convolution_bitcast_fusion.1), channel_id=1, replica_groups=mesh['example'=64,'feature'=4] {'feature'}, use_global_device_ids=true, to_apply=%region_7.9 | all-reduce | flops 73728 | bytes 442368 | tf_op jit(solution)/shard_map/psum | solution.py:77
  783.8 1.4 fusion.49
  785.3 3.6 add_convert_fusion
  (32 shorter events, 2.9 us)
Async XLA Ops:
  6.5 29.5 %copy-start = (s32[4096,128]{1,0:T(8,128)S(1)}, s32[4096,128]{1,0:T(8,128)}, u32[]{:S(2)}) copy-start(s32[4096,128]{1,0:T(8,128)} %param.7) | copy-start | bytes 6291460
  6.5 169.5 %reduce-scatter.4.cloned.1.call-start = ((), (), s32[]{:S(2)}) async-start(), calls=%async_computation.4 | async-start | bytes 2129920
  33.0 3.2 copy-start.3
  35.9 388.0 %all-reduce.5.cloned.1.call-start = ((), (), s32[]{:S(2)}) async-start(), calls=%async_computation.1 | async-start | bytes 131072 | tf_op jit(solution)/shard_map/psum | solution.py:63
  177.8 506.8 %all-reduce.7.cloned.1.call-start = ((), (), s32[]{:S(2)}) async-start(), calls=%async_computation.2 | async-start | bytes 131072 | tf_op jit(solution)/shard_map/psum | solution.py:66
  450.2 311.2 %all-gather.2.cloned.1.call-start = ((), (), s32[]{:S(2)}) async-start(), calls=%async_computation.3 | async-start | bytes 1064960 | tf_op jit(solution)/shard_map/all_gather | solution.py:76
  761.4 22.4 %copy-start.1 = (bf16[4096,128]{1,0:T(8,128)(2,1)S(1)}, bf16[4096,128]{1,0:T(8,128)(2,1)}, u32[]{:S(2)}) copy-start(bf16[4096,128]{1,0:T(8,128)(2,1)} %all-gather.2.cloned.1.call-done) | copy-start | bytes 3145732
  783.8 1.4 copy-start.2
Sparse Core Ops, SparseCore 0:
  36.1 139.8 reduce-scatter.3
  182.4 241.5 all-reduce.4
  450.3 234.2 all-reduce.6
  688.5 72.8 all-gather.1
where the time goes:
time: 798 us; the launch traced here: 795 us
  waiting for transfers between devices  678 us (85%)
  other arithmetic  38.4 us (5%)
  blocking collectives  34.8 us (4%)
  matrix products  25.4 us (3%)
  between operations  13.3 us (2%)
    psum x1, waiting for transfers between devices, on_device(): lax.psum(transposed(image, image, HIGH), ('example', 'feature'))  246 us
    psum x1, waiting for transfers between devices, on_device(): lax.psum(transposed(orthonormal * row_counts[:, None], orthonormal, HIGH)...  234 us
    unnamed x5, waiting for transfers between devices  125 us
    all_gather x1, waiting for transfers between devices, on_device(): grad_low = lax.all_gather(grad_low, 'example', axis=0, tiled=True)  73 us
    another operation x5, other arithmetic, upper_factor(): return jnp.linalg.cholesky(gram_matrix).T  22.8 us
    psum x1, blocking collectives, on_device(): lax.psum(jnp.dot(embeddings, subspace, preferred_element_type=jnp.float32...  17.6 us
    psum x1, blocking collectives, on_device(): lax.psum(jnp.dot(embeddings, grad_low, preferred_element_type=jnp.float32...  17.2 us
  transfers between devices with their start and end apart: 4, of which 4 were waited for; matrix products, arithmetic and copies ran while one was open for 2% of the time, Pallas kernels for 0%

commit v1 on v0

v1 whole, which is shorter than its diff:
```python
import functools

import jax
import jax.numpy as jnp
from jax import lax
from jax.experimental import pallas as pl
from jax.experimental.pallas import tpu as pltpu
from jax.sharding import PartitionSpec as P

MESH = pl.DeviceIdType.MESH
NOISE_STEP = 1.0 / 4096.0
HIGH = lax.Precision.HIGHEST
F32 = jnp.float32
BF16 = jnp.bfloat16
K = 128
H = K // 2
NT = (((1,), (1,)), ((), ()))


def far_first(n):
    return sorted(range(1, n), key=lambda d: -min(d, n - d))


def invert(a):
    lane = lax.broadcasted_iota(jnp.int32, (8, K), 1)
    row = lax.broadcasted_iota(jnp.int32, (8, K), 0)
    blocks = [a[8 * i : 8 * i + 8, :] for i in range(K // 8)]
    for p in range(K // 8):
        r = blocks[p]
        cols = [jnp.broadcast_to(r[:, 8 * p + j : 8 * p + j + 1], (8, K)) for j in range(8)]
        for j in range(8):
            k = 8 * p + j
            cj = cols[j]
            inv = 1.0 / jnp.broadcast_to(cj[j : j + 1, :], (8, K))
            y = jnp.where(lane == k, inv, jnp.broadcast_to(r[j : j + 1, :], (8, K)) * inv)
            r = jnp.where(row == j, y, jnp.where(lane == k, 0.0, r) - cj * y)
            for m in range(j + 1, 8):
                ym = jnp.broadcast_to(cols[m][j : j + 1, :], (8, K)) * inv
                cols[m] = jnp.where(row == j, ym, cols[m] - cj * ym)
        rows = [jnp.broadcast_to(r[j : j + 1, :], (8, K)) for j in range(8)]
        in_panel = (lane >= 8 * p) & (lane < 8 * p + 8)
        for i in range(K // 8):
            if i == p:
                continue
            b = blocks[i]
            total = jnp.where(in_panel, 0.0, b)
            for j in range(8):
                total = total - jnp.broadcast_to(b[:, 8 * p + j : 8 * p + j + 1], (8, K)) * rows[j]
            blocks[i] = total
        blocks[p] = r
    return jnp.concatenate(blocks, axis=0)


def split(v):
    hi = v.astype(BF16)
    return hi, (v - hi.astype(F32)).astype(BF16)


def kernel(X, Y, Z, total_rows, e_hbm, s_hbm, n_hbm, t_ref, pb_out, g_out,
           ebuf, sbuf, nbuf, ntr, cnt, cntb, e_sem, s_sem, n_sem, g_sem,
           ps, pr, plow, bs, br, blow, pt, ptp,
           u, cs, cr, xs, xr, zs, zr, imt, imn, itr,
           g, gr, gq, gpr, gfull, grad,
           p_ss, p_rs, pa_ss, pa_rs, b_ss, b_rs, ba_ss, ba_rs,
           c_ss, c_rs, x_ss, x_rs, z_ss, z_rs, h_ss, h_rs,
           gz_ss, gz_rs, gp_ss, gp_rs, ga_ss, ga_rs,
           az_ss, az_rs, ax_ss, ax_rs, ac_ss, ac_rs):
    R, W = ebuf.shape
    RC = R // Y
    CX = W // X
    GB = K // Z
    e = lax.axis_index("example")
    y = lax.axis_index("feature")
    x = e // (2 * Z)
    z = lax.rem(e // 2, Z)
    c = lax.rem(e, 2)

    def peer(dx=0, dy=0, dz=0, dc=0):
        px = lax.rem(x + dx, X)
        py = lax.rem(y + dy, Y)
        pz = lax.rem(z + dz, Z)
        pc = lax.rem(c + dc, 2)
        return ((px * Z + pz) * 2 + pc, py)

    def remote(src, dst, ss, rs, to):
        return pltpu.make_async_remote_copy(
            src_ref=src, dst_ref=dst, send_sem=ss, recv_sem=rs, device_id=to, device_id_type=MESH
        )

    sent = []

    def send(src, dst, ss, rs, to):
        copy = remote(src, dst, ss, rs, to)
        copy.start()
        sent.append(copy)
        return copy

    plane = [(dx, dy) for dx in range(X) for dy in range(Y) if (dx, dy) != (0, 0)]
    column = [(dz, dc) for dz in range(Z) for dc in range(2) if (dz, dc) != (0, 0)]

    s_copy = pltpu.make_async_copy(s_hbm, sbuf, s_sem)
    s_copy.start()
    y_order = far_first(Y) + [0]
    e_copies = {}
    for d in y_order:
        rows = pl.ds(pl.multiple_of(lax.rem(y + d, Y) * RC, 16), RC)
        e_copies[d] = pltpu.make_async_copy(e_hbm.at[rows], ebuf.at[rows], e_sem.at[d])
        e_copies[d].start()
    block = x * Z + z
    n_copy = pltpu.make_async_copy(n_hbm.at[pl.ds(pl.multiple_of(block * K, K), K)], nbuf, n_sem)
    n_copy.start()

    barrier = pltpu.get_barrier_semaphore()
    for dx, dy in plane:
        pl.semaphore_signal(barrier, inc=1, device_id=peer(dx=dx, dy=dy), device_id_type=MESH)
    for dz, dc in column:
        pl.semaphore_signal(barrier, inc=1, device_id=peer(dz=dz, dc=dc), device_id_type=MESH)

    s_copy.wait()
    first = True
    own = None
    for d in y_order:
        rows = pl.ds(pl.multiple_of(lax.rem(y + d, Y) * RC, 16), RC)
        e_copies[d].wait()
        part = jnp.dot(ebuf[rows, :], sbuf[...], preferred_element_type=F32)
        if d:
            ps[d - 1] = part.astype(BF16)
            if first:
                pl.semaphore_wait(barrier, len(plane) + len(column))
                first = False
            send(ps.at[d - 1], pr.at[d - 1], p_ss.at[d - 1], p_rs.at[d - 1], peer(dy=d))
        else:
            own = part

    t = t_ref[...]
    hi = lax.broadcasted_iota(jnp.int32, (W // K, t.shape[1]), 0) + y * (W // K)
    lo = lax.broadcasted_iota(jnp.int32, (K, t.shape[1]), 0)
    hot_hi = jnp.where(hi == t // K, 1.0, 0.0).astype(BF16)
    hot_lo = jnp.where(lo == lax.rem(t, K), 1.0, 0.0).astype(BF16)
    cnt[...] = lax.dot_general(hot_hi, hot_lo, NT, preferred_element_type=F32)
    n_copy.wait()
    ntr[...] = (NOISE_STEP * nbuf[...].astype(F32)).T

    my_rows = pl.ds(pl.multiple_of(y * RC, 16), RC)
    for d in range(1, Y):
        remote(ps.at[d - 1], pr.at[d - 1], p_ss.at[d - 1], p_rs.at[d - 1], peer(dy=d)).wait_recv()
        own = own + pr[d - 1].astype(F32)
    plow[my_rows, :] = own.astype(BF16)
    for d in far_first(Y):
        send(plow.at[my_rows], plow.at[my_rows], pa_ss.at[d - 1], pa_rs.at[d - 1], peer(dy=d))
    cnt_cols = lax.dot_general(hot_lo, hot_hi, NT, preferred_element_type=F32)
    for b in range(W // K):
        cntb[b] = jnp.broadcast_to(cnt_cols[:, b : b + 1], (K, K))
    for d in range(1, Y):
        rows = pl.ds(pl.multiple_of(lax.rem(y + Y - d, Y) * RC, 16), RC)
        remote(plow.at[rows], plow.at[rows], pa_ss.at[d - 1], pa_rs.at[d - 1], peer(dy=d)).wait_recv()

    pt[...] = plow[...].T
    ptp[0:H, :] = pt[pl.ds(pl.multiple_of(c * H, H), H), :]
    ptp[H:K, :] = pt[pl.ds(pl.multiple_of((1 - c) * H, H), H), :]
    x_order = far_first(X) + [0]

    def pass_on(d):
        remote(cs.at[d], cr.at[d], c_ss.at[d], c_rs.at[d], peer(dc=1)).wait_recv()
        v = u[d] + cr[d].astype(F32)
        if d:
            xs[d - 1] = v.astype(BF16)
            send(xs.at[d - 1], xr.at[d - 1], x_ss.at[d - 1], x_rs.at[d - 1], peer(dx=d))
        else:
            u[0] = v

    before = None
    for d in x_order:
        cols = pl.ds(pl.multiple_of(lax.rem(x + d, X) * CX, K), CX)
        part = jnp.dot(ptp[...], ebuf[:, cols], preferred_element_type=F32)
        cs[d] = part[H:K].astype(BF16)
        send(cs.at[d], cr.at[d], c_ss.at[d], c_rs.at[d], peer(dc=1))
        u[d] = part[0:H]
        if before is not None:
            pass_on(before)
        before = d
    pass_on(before)
    for d in range(1, X):
        remote(xs.at[d - 1], xr.at[d - 1], x_ss.at[d - 1], x_rs.at[d - 1], peer(dx=d)).wait_recv()
    total = None
    for d in far_first(Z) + [0]:
        cols = pl.ds(pl.multiple_of(lax.rem(z + d, Z) * K, K), K)
        v = u[0, :, cols]
        for dx in range(1, X):
            v = v + xr[dx - 1, :, cols].astype(F32)
        if d:
            zs[d - 1] = v.astype(BF16)
            send(zs.at[d - 1], zr.at[d - 1], z_ss.at[d - 1], z_rs.at[d - 1], peer(dz=d))
        else:
            total = v
    for d in range(1, Z):
        remote(zs.at[d - 1], zr.at[d - 1], z_ss.at[d - 1], z_rs.at[d - 1], peer(dz=d)).wait_recv()
        total = total + zr[d - 1].astype(F32)
    half = pl.ds(pl.multiple_of(c * H, H), H)
    other = pl.ds(pl.multiple_of((1 - c) * H, H), H)
    imt[half, :] = total / total_rows + ntr[half, :]
    send(imt.at[half], imt.at[half], h_ss, h_rs, peer(dc=1))
    remote(imt.at[other], imt.at[other], h_ss, h_rs, peer(dc=1)).wait_recv()

    im = imt[...]
    weight = jnp.where(c == 0, 1.0, cnt[pl.ds(block, 1), :])
    g[...] = lax.dot_general(im * weight, im, NT, precision=HIGH, preferred_element_type=F32)
    for d in far_first(Z):
        rows = pl.ds(pl.multiple_of(lax.rem(z + d, Z) * GB, 8), GB)
        send(g.at[rows], gr.at[d - 1], gz_ss.at[d - 1], gz_rs.at[d - 1], peer(dz=d))
    itr[...] = im.T
    imn[block, c] = itr[half, :]
    mine = pl.ds(pl.multiple_of(z * GB, 8), GB)
    v = g[mine, :]
    for d in range(1, Z):
        remote(gr.at[d - 1], gr.at[d - 1], gz_ss.at[d - 1], gz_rs.at[d - 1], peer(dz=d)).wait_recv()
        v = v + gr[d - 1]
    gq[...] = v
    for i, (dx, dy) in enumerate(plane):
        send(gq, gpr.at[i], gp_ss.at[i], gp_rs.at[i], peer(dx=dx, dy=dy))
    for i, (dx, dy) in enumerate(plane):
        remote(gq, gpr.at[i], gp_ss.at[i], gp_rs.at[i], peer(dx=dx, dy=dy)).wait_recv()
        v = v + gpr[i]
    gfull[c, mine, :] = v
    for i, (dz, dc) in enumerate(column):
        send(gfull.at[c, mine], gfull.at[c, mine], ga_ss.at[i], ga_rs.at[i], peer(dz=dz, dc=dc))

    for d in far_first(Z):
        send(imn.at[block, c], imn.at[block, c], az_ss.at[d - 1], az_rs.at[d - 1], peer(dz=d))

    for i, (dz, dc) in enumerate(column):
        sc = lax.rem(c + dc, 2)
        rows = pl.ds(pl.multiple_of(lax.rem(z + Z - dz, Z) * GB, 8), GB)
        remote(gfull.at[sc, rows], gfull.at[sc, rows], ga_ss.at[i], ga_rs.at[i], peer(dz=dz, dc=dc)).wait_recv()
    for d in range(1, Z):
        b = x * Z + lax.rem(z + Z - d, Z)
        remote(imn.at[b, c], imn.at[b, c], az_ss.at[d - 1], az_rs.at[d - 1], peer(dz=d)).wait_recv()
    slab = pl.ds(x * Z, Z)
    for d in far_first(X):
        send(imn.at[slab, c], imn.at[slab, c], ax_ss.at[d - 1], ax_rs.at[d - 1], peer(dx=d))
    send(imn.at[slab, c], imn.at[slab, c], ac_ss.at[0], ac_rs.at[0], peer(dc=1))

    inv = invert(gfull[0])
    mid = jnp.dot(inv, gfull[1], precision=HIGH, preferred_element_type=F32)
    mid = jnp.dot(mid, inv, precision=HIGH, preferred_element_type=F32)
    both_hi, both_lo = split(2.0 * jnp.concatenate([mid, inv], axis=1))

    for d in range(1, X):
        there = pl.ds(lax.rem(x + X - d, X) * Z, Z)
        remote(imn.at[there, c], imn.at[there, c], ax_ss.at[d - 1], ax_rs.at[d - 1], peer(dx=d)).wait_recv()
        send(imn.at[there, c], imn.at[there, c], ac_ss.at[d], ac_rs.at[d], peer(dc=1))
    for d in range(X):
        there = pl.ds(lax.rem(x + X - d, X) * Z, Z)
        remote(imn.at[there, 1 - c], imn.at[there, 1 - c], ac_ss.at[d], ac_rs.at[d], peer(dc=1)).wait_recv()

    for b in range(W // K):
        a_hi, a_lo = split(imn[b].reshape(K, K))
        v = jnp.dot(a_hi, both_hi, preferred_element_type=F32)
        v = v + jnp.dot(a_hi, both_lo, preferred_element_type=F32)
        v = v + jnp.dot(a_lo, both_hi, preferred_element_type=F32)
        grad[b * K : (b + 1) * K, :] = (v[:, :K] - cntb[b] * v[:, K:]).astype(BF16)
    g_copy = pltpu.make_async_copy(grad, g_out, g_sem)
    g_copy.start()

    for d in y_order:
        rows = pl.ds(pl.multiple_of(lax.rem(y + d, Y) * RC, 16), RC)
        part = jnp.dot(ebuf[rows, :], grad[...], preferred_element_type=F32)
        if d:
            bs[d - 1] = part.astype(BF16)
            send(bs.at[d - 1], br.at[d - 1], b_ss.at[d - 1], b_rs.at[d - 1], peer(dy=d))
        else:
            own = part
    for d in range(1, Y):
        remote(bs.at[d - 1], br.at[d - 1], b_ss.at[d - 1], b_rs.at[d - 1], peer(dy=d)).wait_recv()
        own = own + br[d - 1].astype(F32)
    blow[my_rows, :] = own.astype(BF16)
    for d in far_first(Y):
        send(blow.at[my_rows], blow.at[my_rows], ba_ss.at[d - 1], ba_rs.at[d - 1], peer(dy=d))
    pb_out[:, 0:K] = plow[...]
    for d in range(1, Y):
        rows = pl.ds(pl.multiple_of(lax.rem(y + Y - d, Y) * RC, 16), RC)
        remote(blow.at[rows], blow.at[rows], ba_ss.at[d - 1], ba_rs.at[d - 1], peer(dy=d)).wait_recv()
    pb_out[:, K:] = blow[...]

    for copy in sent:
        copy.wait_send()
    g_copy.wait()


def output_kernel(pb_ref, g_ref, s_ref, out_ref):
    both = jnp.concatenate([g_ref[...], s_ref[...]], axis=1)
    out_ref[...] = lax.dot_general(pb_ref[...], both, NT, preferred_element_type=F32).astype(BF16)


def make(X, Y, Z):
    def on_device(embeddings, subspace, noise_levels, targets):
        R, W = embeddings.shape
        RC, CX, B = R // Y, W // X, W // K
        dma = pltpu.SemaphoreType.DMA
        V = pltpu.VMEM
        any_spec = pl.BlockSpec(memory_space=pl.ANY)
        vmem_spec = pl.BlockSpec(memory_space=pltpu.VMEM)

        def sems(*counts):
            return [dma((n,)) for n in counts]

        pb, grad = pl.pallas_call(
            functools.partial(kernel, X, Y, Z, float(R * X * Z * 2)),
            out_shape=(jax.ShapeDtypeStruct((R, 2 * K), BF16), jax.ShapeDtypeStruct((W, K), BF16)),
            in_specs=[any_spec, any_spec, any_spec, vmem_spec],
            out_specs=(vmem_spec, any_spec),
            scratch_shapes=[
                V((R, W), BF16), V((W, K), BF16), V((K, K), jnp.int32), V((K, K), F32),
                V((B, K), F32), V((B, K, K), F32),
                dma((Y,)), dma, dma, dma,
                V((Y - 1, RC, K), BF16), V((Y - 1, RC, K), BF16), V((R, K), BF16),
                V((Y - 1, RC, K), BF16), V((Y - 1, RC, K), BF16), V((R, K), BF16),
                V((K, R), BF16), V((K, R), BF16),
                V((X, H, CX), F32), V((X, H, CX), BF16), V((X, H, CX), BF16),
                V((X - 1, H, CX), BF16), V((X - 1, H, CX), BF16),
                V((Z - 1, H, K), BF16), V((Z - 1, H, K), BF16),
                V((K, K), F32), V((B, 2, H, K), F32), V((K, K), F32),
                V((K, K), F32), V((Z - 1, K // Z, K), F32), V((K // Z, K), F32),
                V((X * Y - 1, K // Z, K), F32), V((2, K, K), F32), V((W, K), BF16),
                *sems(Y - 1, Y - 1, Y - 1, Y - 1, Y - 1, Y - 1, Y - 1, Y - 1),
                *sems(X, X, X - 1, X - 1, Z - 1, Z - 1), dma, dma,
                *sems(Z - 1, Z - 1, X * Y - 1, X * Y - 1, 2 * Z - 1, 2 * Z - 1),
                *sems(Z - 1, Z - 1, X - 1, X - 1, X, X),
            ],
            compiler_params=pltpu.CompilerParams(
                collective_id=0, has_side_effects=True, vmem_limit_bytes=50 * 2**20
            ),
        )(embeddings, subspace, noise_levels, targets.reshape(1, -1))

        tile = min(512, W)
        return pl.pallas_call(
            output_kernel,
            grid=(W // tile,),
            out_shape=jax.ShapeDtypeStruct((R, W), BF16),
            in_specs=[
                pl.BlockSpec((R, 2 * K), lambda i: (0, 0)),
                pl.BlockSpec((tile, K), lambda i: (i, 0)),
                pl.BlockSpec((tile, K), lambda i: (i, 0)),
            ],
            out_specs=pl.BlockSpec((R, tile), lambda i: (0, i)),
        )(pb, grad, subspace)

    return on_device


def solution(mesh, X=4, Z=8):
    in_specs = (P("example", "feature"), P("feature", None), P("feature", None), P())
    return jax.shard_map(
        make(X, mesh.shape["feature"], Z),
        mesh=mesh,
        in_specs=in_specs,
        out_specs=P("example", "feature"),
        check_vma=False,
    )
```

time: 798 us -> 95.8 us (0.12)
  waiting for transfers between devices: 678 us -> 0 us
  Pallas kernels: 0 us -> 91.9 us
  other arithmetic: 38.4 us -> 0 us
  blocking collectives: 34.8 us -> 0 us
  matrix products: 25.4 us -> 0 us
  between operations: 13.3 us -> 0.02 us
    psum x2 -> x0, waiting for transfers between devices: 480 us -> none  [the longest x1 246 us: on_device(): lax.psum(transposed(image, image, HIGH), ('example', 'feature'))]
    unnamed x5 -> x0, waiting for transfers between devices: 125 us -> none
    pallas_call x0 -> x2, Pallas kernels: none -> 91.9 us  [the longest x1 84.4 us: on_device(): pl.pallas_call(functools.partial(kernel, X, Y, Z, float(R * X * Z * 2)),...]
    all_gather x1 -> x0, waiting for transfers between devices: 73 us -> none  [on_device(): grad_low = lax.all_gather(grad_low, 'example', axis=0, tiled=True)]
    psum x2 -> x0, blocking collectives: 34.8 us -> none  [the longest x1 17.6 us: on_device(): lax.psum(jnp.dot(embeddings, subspace, preferred_element_type=jnp.float32...]
    dot_general x13 -> x0, matrix products: 24.7 us -> none  [the longest x3 6.56 us: transposed(): lax.dot_general(former, latter, (((0,), (0,)), ((), ())), precision=preci...]
    another operation x5 -> x0, other arithmetic: 22.8 us -> none  [upper_factor(): return jnp.linalg.cholesky(gram_matrix).T]
    scatter-add x1 -> x0, other arithmetic: 14.7 us -> none  [count_rows(): return jax.ops.segment_sum(ones, slots, num_segments=length + 1)[:length]]
  transfers between devices with their start and end apart: 4 -> 0, of which waited for: 4 -> 0; matrix products, arithmetic and copies ran while one was open for 2% -> 0% of each run, Pallas kernels for 0% -> 0%
where the time goes in v1:
time: 95.8 us; the launch traced here: 95.5 us
  Pallas kernels  91.9 us (96%)
  local copies, waits for them, and re-layouts  3.59 us (4%)
    pallas_call x1, Pallas kernels, on_device(): pl.pallas_call(functools.partial(kernel, X, Y, Z, float(R * X * Z * 2)),...  84.4 us
    pallas_call x1, Pallas kernels, on_device(): pl.pallas_call(output_kernel, grid=(W // tile,), out_shape=jax.ShapeDtype...  7.54 us
    unnamed x8, local copies, waits for them, and re-layouts  3.59 us

profile of v1, /device:TPU:1, one launch (start us, length us, event | category | flops | bytes accessed | tf_op | source)
XLA Modules:
  0.0 95.5 jit_solution(7160903350449103884)
XLA Ops:
  0.0 0.0 copy-start
  0.0 1.2 %copy-done = bf16[4096,128]{1,0:T(8,128)(2,1)S(1)} copy-done((bf16[4096,128]{1,0:T(8,128)(2,1)S(1)}, bf16[4096,128]{1,0:T(8,128)(2,1)}, u32[]{:S(2)}) %copy-start) | copy-done | bytes 1048600
  1.2 0.0 copy-start.3
  1.2 0.7 copy-done.3
  1.9 84.4 %shard_map.46 = (bf16[576,256]{1,0:T(8,128)(2,1)S(1)}, bf16[4096,128]{1,0:T(8,128)(2,1)S(1)}) custom-call(bf16[576,4096]{1,0:T(8,128)(2,1)} %e_hbm.1, bf16[4096,128]{1,0:T(8,128)(2,1)S(1)} %copy-done, s32[4096,128]{1,0:T(8,128)} %n_hbm.1, s32[1,2048]{1,0:T(1,128)S(1)} %bitcast.1), custom_call_target="tpu_custom_call" | custom-call | tf_op jit(solution)/shard_map/pallas_call | solution.py:307
  86.3 0.0 copy-start.1
  86.3 1.0 %copy-done.1 = bf16[4096,128]{1,0:T(8,128)(2,1)} copy-done((bf16[4096,128]{1,0:T(8,128)(2,1)}, bf16[4096,128]{1,0:T(8,128)(2,1)S(1)}, u32[]{:S(2)}) %copy-start.1) | copy-done | bytes 1048600
  87.3 0.0 copy-start.2
  87.3 0.7 copy-done.2
  88.0 7.5 %shard_map.47 = bf16[576,4096]{1,0:T(8,128)(2,1)} custom-call(bf16[576,256]{1,0:T(8,128)(2,1)} %copy-done.2, bf16[4096,128]{1,0:T(8,128)(2,1)} %copy-done.1, bf16[4096,128]{1,0:T(8,128)(2,1)} %s_ref.1), custom_call_target="tpu_custom_call" | custom-call | tf_op jit(solution)/shard_map/pallas_call | solution.py:336
Async XLA Ops:
  0.0 1.2 %copy-start = (bf16[4096,128]{1,0:T(8,128)(2,1)S(1)}, bf16[4096,128]{1,0:T(8,128)(2,1)}, u32[]{:S(2)}) copy-start(bf16[4096,128]{1,0:T(8,128)(2,1)} %s_ref.1) | copy-start | bytes 3145732
  1.2 0.7 copy-start.3
  86.3 1.0 %copy-start.1 = (bf16[4096,128]{1,0:T(8,128)(2,1)}, bf16[4096,128]{1,0:T(8,128)(2,1)S(1)}, u32[]{:S(2)}) copy-start(bf16[4096,128]{1,0:T(8,128)(2,1)S(1)} %get-tuple-element.8.g_ref) | copy-start | bytes 3145732
  87.3 0.7 copy-start.2
